TPU v7x, 32 devices: a whole 2x2x4 slice. The times are simulated.
32 devices in a mesh: ctx: 8 (over y, x, core), head: 4 (over z).
Axes of the slice: x: 2, y: 2, z: 4, core: 2. Of those that a mesh axis runs over, the one named last changes fastest.
Arguments:
- inputs: bfloat16 [4096, 4096], P('ctx'), may hold values from -8 to 8
- query_weight: bfloat16 [4096, 2048], P(None, 'head'), may hold values from -0.09375 to 0.09375
- key_weight: bfloat16 [4096, 512], P(None, 'head'), may hold values from -0.09375 to 0.09375
- value_weight: bfloat16 [4096, 512], P(None, 'head'), may hold values from -0.09375 to 0.09375
- out_grad: bfloat16 [4096, 2048], P('ctx', 'head'), may hold values from -6 to 6
- doc_lengths: int32 [8], replicated, may hold values from 128 to 1536, as said below
Outputs:
- attn_out: bfloat16 [4096, 2048], P('ctx', 'head')
- input_grad: bfloat16 [4096, 4096], P('ctx', 'head')
- query_weight_grad: float32 [4096, 2048], P('ctx', 'head')
- key_weight_grad: float32 [4096, 512], P('ctx', 'head')
- value_weight_grad: float32 [4096, 512], P('ctx', 'head')
Inputs may be any that keep to these rules, and one draw needn't show every extreme that they name: `doc_lengths`: each length is a positive multiple of 128; the lengths sum to 4096; the largest is exactly 1536.
All inputs are finite; a program needn't handle non-finite values.
Results may differ from a plain program's by a relative error of at most 0.018.
The roundings to bfloat16 on the way count: a program that leaves them out, or rounds other values in their place, can miss the bound.
Values may be sent and summed in bfloat16 or wider, within the bound.
No kernel may reach another device: no remote copies, remote signals or barrier semaphores. Data moves between devices by JAX's collectives and lax.ppermute only.
A program may use at most 128 MiB of HBM per device.

v0:
```python
from functools import partial

import jax
import jax.numpy as jnp
from jax import lax
from jax.experimental import pallas as pl
from jax.experimental.pallas import tpu as pltpu
from jax.sharding import PartitionSpec as P

HD = 128
GROUP = 4
SPAN = 3
GRAIN = 128
TILE = 256

NEG = -1e30
LOG2E = 1.4426950408889634


def dot_nt(left_mat, right_mat):
    return lax.dot_general(
        left_mat, right_mat, (((1,), (1,)), ((), ())), preferred_element_type=jnp.float32
    )


def dot_tn(left_mat, right_mat):
    return lax.dot_general(
        left_mat, right_mat, (((0,), (0,)), ((), ())), preferred_element_type=jnp.float32
    )


def dot_nn(left_mat, right_mat):
    return jnp.dot(left_mat, right_mat, preferred_element_type=jnp.float32)


def attention_kernel(
    first_ref, query_ref, grad_ref, kv0, kv1, kv2, kv3,
    out_ref, dq_ref, d0, d1, d2, d3,
    kv_ref, acc_ref, score_ref,
):
    rows = query_ref.shape[0]
    for slot, block in enumerate((kv3, kv2, kv1, kv0)):
        kv_ref[pl.ds(slot * rows, rows), :] = block[...]
    acc_ref[...] = jnp.zeros_like(acc_ref)
    factor = HD ** (-0.5)
    wide = GROUP * GRAIN
    for granule in range(rows // GRAIN):
        here = pl.ds(granule * GRAIN, GRAIN)
        heads = [slice(h * HD, (h + 1) * HD) for h in range(GROUP)]
        query = jnp.concatenate([query_ref[here, cols] for cols in heads], axis=0)
        grad = jnp.concatenate([grad_ref[here, cols] for cols in heads], axis=0)
        own = SPAN * rows + granule * GRAIN
        last = own // TILE
        first_key = first_ref[granule]
        low = first_key // TILE

        def tile_rows(tile):
            return pl.ds(pl.multiple_of(tile * TILE, TILE), TILE)

        def score_tile(tile, top, diagonal):
            score = dot_nt(kv_ref[tile_rows(tile), :HD], query) * (factor * LOG2E)
            key_pos = tile * TILE + lax.broadcasted_iota(jnp.int32, (TILE, wide), 0)
            keep = key_pos >= first_key
            if diagonal:
                query_pos = own + lax.broadcasted_iota(jnp.int32, (TILE, wide), 1) % GRAIN
                keep = keep & (key_pos <= query_pos)
            score = jnp.where(keep, score, NEG)
            score_ref[tile_rows(tile), :] = score
            return jnp.maximum(top, jnp.max(score.reshape(TILE // 8, 8, wide), axis=0))

        top = lax.fori_loop(
            low, last, lambda tile, top: score_tile(tile, top, False),
            jnp.full((8, wide), NEG, jnp.float32),
        )
        top = score_tile(last, top, True)
        top = jnp.max(top, axis=0, keepdims=True)

        def weight_tile(tile, total):
            weight = jnp.exp2(score_ref[tile_rows(tile), :] - top)
            score_ref[tile_rows(tile), :] = weight
            return total + jnp.sum(weight.reshape(TILE // 8, 8, wide), axis=0)

        total = lax.fori_loop(low, last + 1, weight_tile, jnp.zeros((8, wide), jnp.float32))
        inverse = 1.0 / jnp.sum(total, axis=0, keepdims=True)

        def output_tile(tile, accum):
            prob = (score_ref[tile_rows(tile), :] * inverse).astype(jnp.bfloat16)
            acc_ref[tile_rows(tile), HD:] += dot_nn(prob, grad)
            return accum + dot_tn(kv_ref[tile_rows(tile), HD:], prob)

        accum = lax.fori_loop(low, last + 1, output_tile, jnp.zeros((HD, wide), jnp.float32))
        out = accum.T.astype(jnp.bfloat16)
        delta = jnp.sum(
            (out.astype(jnp.float32) * grad.astype(jnp.float32)).T, axis=0, keepdims=True
        )

        def grad_tile(tile, accum):
            prob = score_ref[tile_rows(tile), :] * inverse
            dprob = dot_nt(kv_ref[tile_rows(tile), HD:], grad)
            dscore = (prob * (dprob - delta)).astype(jnp.bfloat16)
            acc_ref[tile_rows(tile), :HD] += dot_nn(dscore, query)
            return accum + dot_tn(kv_ref[tile_rows(tile), :HD], dscore)

        accum = lax.fori_loop(low, last + 1, grad_tile, jnp.zeros((HD, wide), jnp.float32))
        dquery = (accum * factor).T.astype(jnp.bfloat16)
        for head, cols in enumerate(heads):
            part = slice(head * GRAIN, (head + 1) * GRAIN)
            out_ref[here, cols] = out[part]
            dq_ref[here, cols] = dquery[part]
    for slot, block in enumerate((d3, d2, d1, d0)):
        place = pl.ds(slot * rows, rows)
        block[:, :HD] = acc_ref[place, :HD] * factor
        block[:, HD:] = acc_ref[place, HD:]


def attention(first, query, grad, kv_list):
    rows, cols = query.shape
    window = (SPAN + 1) * rows
    low = jax.ShapeDtypeStruct((rows, cols), jnp.bfloat16)
    high = jax.ShapeDtypeStruct((rows, 2 * HD), jnp.float32)
    vmem = pl.BlockSpec(memory_space=pltpu.VMEM)
    return pl.pallas_call(
        attention_kernel,
        out_shape=(low, low) + (high,) * (SPAN + 1),
        in_specs=[pl.BlockSpec(memory_space=pltpu.SMEM)] + [vmem] * (SPAN + 3),
        out_specs=(vmem,) * (SPAN + 3),
        scratch_shapes=[
            pltpu.VMEM((window, 2 * HD), jnp.bfloat16),
            pltpu.VMEM((window, 2 * HD), jnp.float32),
            pltpu.VMEM((window, GROUP * GRAIN), jnp.float32),
        ],
        compiler_params=pltpu.CompilerParams(vmem_limit_bytes=32 * 1024 * 1024),
        cost_estimate=pl.CostEstimate(
            flops=6 * 2 * rows * window * cols, bytes_accessed=6 * 2**20, transcendentals=0
        ),
        name="attention",
    )(first, query, grad, *kv_list)


def shift(value, axis, steps):
    count = lax.axis_size(axis)
    pairs = [(i, i + steps) for i in range(count) if 0 <= i + steps < count]
    return lax.ppermute(value, axis, pairs)


def swap(value, axis, mask):
    return lax.ppermute(value, axis, [(i, i ^ mask) for i in range(lax.axis_size(axis))])


def rotate(value, axis, steps):
    count = lax.axis_size(axis)
    return lax.ppermute(value, axis, [(i, (i + steps) % count) for i in range(count)])


def body(inputs, query_weight, key_weight, value_weight, out_grad, doc_lengths):
    tok_rows, width = inputs.shape
    n_ctx = lax.axis_size("ctx")
    n_head = lax.axis_size("head")
    chips = n_ctx // 2
    ctx = lax.axis_index("ctx")
    head = lax.axis_index("head")
    q_cols = query_weight.shape[1]
    k_cols = key_weight.shape[1]
    weights = (query_weight, key_weight, value_weight)

    kv_loc = jnp.concatenate(
        [dot_nn(inputs, key_weight).astype(jnp.bfloat16), dot_nn(inputs, value_weight).astype(jnp.bfloat16)],
        axis=1,
    )
    kv_list = [kv_loc] + [shift(kv_loc, "ctx", distance) for distance in range(1, SPAN + 1)]
    query = dot_nn(inputs, query_weight).astype(jnp.bfloat16)

    out_width = width // n_head
    piece = out_width // n_ctx
    weight_rows = []
    for step in range(n_head):
        if step == 0:
            start = head * out_width
            rows = [lax.dynamic_slice_in_dim(w, start, out_width, 0) for w in weights]
            weight_rows.append(jnp.concatenate(rows, axis=1))
            continue
        start = (head + step) % n_head * out_width + ctx * piece
        rows = [lax.dynamic_slice_in_dim(w, start, piece, 0) for w in weights]
        moved = rotate(jnp.concatenate(rows, axis=1), "head", step)
        weight_rows.append(lax.all_gather(moved, "ctx", axis=0, tiled=True))

    split = inputs.reshape(tok_rows, chips, 2, width // n_ctx)
    core = ctx % 2
    own_part = lax.dynamic_index_in_dim(split, core, 2, keepdims=False)
    other_part = lax.dynamic_index_in_dim(split, 1 - core, 2, keepdims=False)
    pair_inputs = jnp.concatenate([own_part, swap(other_part, "ctx", 1)], axis=0)

    granules = tok_rows // GRAIN
    window_start = (ctx - SPAN) * tok_rows
    positions = ctx * tok_rows + GRAIN * jnp.arange(granules, dtype=jnp.int32)
    doc_ends = jnp.cumsum(doc_lengths)
    starts = jnp.sum(
        jnp.where(doc_ends[None, :] <= positions[:, None], doc_lengths[None, :], 0), axis=1
    )
    attn_out, dq_low, *kv_grads = attention(starts - window_start, query, out_grad, kv_list)

    kv_total = kv_grads[0]
    for distance in range(1, SPAN + 1):
        kv_total = kv_total + shift(kv_grads[distance], "ctx", -distance)
    dkv_low = kv_total.astype(jnp.bfloat16)

    grad_sum = jnp.zeros((tok_rows, out_width), jnp.float32)
    moving = (dq_low, dkv_low)
    for step in range(n_head):
        if step > 0:
            moving = tuple(rotate(part, "head", 1) for part in moving)
        rows = weight_rows[step]
        term = dot_nt(moving[0], rows[:, :q_cols]) + dot_nt(moving[1], rows[:, q_cols:])
        grad_sum = grad_sum + term.astype(jnp.bfloat16).astype(jnp.float32)
    input_grad = grad_sum.astype(jnp.bfloat16)

    sums = []
    for low in (dq_low, dkv_low):
        pair = jnp.concatenate([low, swap(low, "ctx", 1)], axis=0)
        total = None
        for chip in range(chips):
            block = lax.dynamic_index_in_dim(pair_inputs, (ctx // 2) ^ chip, 1, keepdims=False)
            term = dot_tn(block, pair)
            if chip > 0:
                term = swap(term.astype(jnp.bfloat16), "ctx", 2 * chip).astype(jnp.float32)
            total = term if total is None else total + term
        sums.append(total)
    return (attn_out, input_grad, sums[0], sums[1][:, :k_cols], sums[1][:, k_cols:])


def solution(mesh):
    return jax.shard_map(
        body,
        mesh=mesh,
        in_specs=(
            P("ctx", None),
            P(None, "head"),
            P(None, "head"),
            P(None, "head"),
            P("ctx", "head"),
            P(),
        ),
        out_specs=(P("ctx", "head"),) * 5,
        check_vma=False,
    )
```

profile of v0, /device:TPU:0, one launch (start us, length us, event | category | flops | bytes accessed | tf_op | source)
XLA Modules:
  0.0 200.9 jit_solution(4524787155807201149)
XLA Ops:
  9.9 4.1 %collective-permute-start.10 = (bf16[128,768]{1,0:T(8,128)(2,1)S(1)}, bf16[128,768]{1,0:T(8,128)(2,1)S(1)}, u32[]{:S(2)}, u32[]{:S(2)}) collective-permute-start(bf16[128,768]{1,0:T(8,128)(2,1)S(1)} %pad_maximum_fusion.3), channel_id=1, source_target_pairs={{0,2},{1,3},{2,0},{3,1},{4,6},{5,7},{6,4},{7,5},{8,10},{9,11},{10,... | collective-permute-start | bytes 589832 | tf_op jit(solution)/shard_map/ppermute | solution.py:152
  14.0 9.1 %collective-permute-done.10 = bf16[128,768]{1,0:T(8,128)(2,1)S(1)} collective-permute-done((bf16[128,768]{1,0:T(8,128)(2,1)S(1)}, bf16[128,768]{1,0:T(8,128)(2,1)S(1)}, u32[]{:S(2)}, u32[]{:S(2)}) %collective-permute-start.10) | collective-permute-done | bytes 196640 | tf_op jit(solution)/shard_map/ppermute | solution.py:152
  24.7 3.8 %convolution_convert_fusion.7 = bf16[512,128]{1,0:T(8,128)(2,1)S(1)} fusion(bf16[512,4096]{1,0:T(8,128)(2,1)} %param.6, bf16[4096,128]{1,0:T(8,128)(2,1)S(1)} %copy-done.21), kind=kOutput, calls=%fused_computation.26 | convolution fusion | flops 536936448 | bytes 5373952 | tf_op jit(solution)/shard_map/dot_general | solution.py:33
  29.8 2.8 %collective-permute-done.7 = bf16[128,768]{1,0:T(8,128)(2,1)S(1)} collective-permute-done((bf16[128,768]{1,0:T(8,128)(2,1)S(1)}, bf16[128,768]{1,0:T(8,128)(2,1)S(1)}, u32[]{:S(2)}, u32[]{:S(2)}) %collective-permute-start.7) | collective-permute-done | bytes 196640 | tf_op jit(solution)/shard_map/ppermute | solution.py:152
  34.7 4.0 %collective-permute-start.1 = (bf16[512,256]{1,0:T(8,128)(2,1)S(1)}, bf16[512,256]{1,0:T(8,128)(2,1)S(1)}, u32[]{:S(2)}, u32[]{:S(2)}) collective-permute-start(bf16[512,256]{1,0:T(8,128)(2,1)S(1)} %pad_maximum_fusion.1.kv0), channel_id=1, source_target_pairs={{0,8},{4,12},{8,16},{12,20},{16,24},{20,28},{1,9},{5,13},{9,17},{1... | collective-permute-start | bytes 786440 | tf_op jit(solution)/shard_map/ppermute | solution.py:143
  38.7 4.3 %collective-permute-start.2 = (bf16[512,256]{1,0:T(8,128)(2,1)S(1)}, bf16[512,256]{1,0:T(8,128)(2,1)S(1)}, u32[]{:S(2)}, u32[]{:S(2)}) collective-permute-start(bf16[512,256]{1,0:T(8,128)(2,1)S(1)} %pad_maximum_fusion.1.kv0), channel_id=1, source_target_pairs={{0,12},{4,16},{8,20},{12,24},{16,28},{1,13},{5,17},{9,21},{13,25},... | collective-permute-start | bytes 786440 | tf_op jit(solution)/shard_map/ppermute | solution.py:143
  43.1 6.5 %copy.22 = bf16[512,4096]{0,1:T(8,128)(2,1)} copy(bf16[512,4096]{1,0:T(8,128)(2,1)} %param.6) | data formatting | bytes 8388608 | tf_op args[0]
  49.6 4.5 %constant_dynamic-slice_fusion = (bf16[512,4,1,512]{0,3,2,1:T(8,128)(2,1)}, bf16[512,4,1,512]{0,3,2,1:T(8,128)(2,1)}) fusion(bf16[512,4,2,512]{0,3,2,1:T(8,128)(2,1)} %bitcast.47, s32[]{:T(128)S(6)} %select_n.88, s32[]{:T(128)S(6)} %select_n.87), kind=kLoop, calls=%fused_computation.58 | loop fusion | bytes 8388616 | tf_op jit(solution)/shard_map/jit(dynamic_index_in_dim)/dynamic_slice | solution.py:190
  54.1 4.2 %copy.24 = bf16[512,4,1,512]{3,0,2,1:T(8,128)(2,1)} copy(bf16[512,4,1,512]{0,3,2,1:T(8,128)(2,1)} %get-tuple-element.17) | data formatting | bytes 4194304 | tf_op jit(solution)/shard_map/jit(dynamic_index_in_dim)/dynamic_slice | solution.py:190
  58.4 6.6 %convolution_convert_fusion.query_ref = bf16[512,512]{1,0:T(8,128)(2,1)} fusion(bf16[512,4096]{1,0:T(8,128)(2,1)} %param.6, bf16[4096,512]{1,0:T(8,128)(2,1)} %param.7), kind=kOutput, calls=%fused_computation.16 | convolution fusion | flops 2147745792 | bytes 8912896 | tf_op jit(solution)/shard_map/dot_general | solution.py:33
  71.3 9.1 %attention.1 = (bf16[512,512]{1,0:T(8,128)(2,1)}, bf16[512,512]{1,0:T(8,128)(2,1)S(1)}, f32[512,256]{1,0:T(8,128)S(1)}, f32[512,256]{1,0:T(8,128)S(1)}, f32[512,256]{1,0:T(8,128)S(1)}, /*index=5*/f32[512,256]{1,0:T(8,128)S(1)}) custom-call(s32[4]{0:T(128)S(1)} %broadcast_subtract_fusion.first_ref, bf16[512,512]{1,0:T(8,128)(2,1)S(1)} %copy-done.7, ...), custom_call_target="tpu_custom_call" | custom-call | flops 6442450944 | bytes 6291456 | tf_op jit(solution)/shard_map/attention/pallas_call | solution.py:122
  84.4 1.8 collective-permute-start.13
  86.2 4.1 %copy.23 = bf16[512,4,1,512]{3,0,2,1:T(8,128)(2,1)} copy(bf16[512,4,1,512]{0,3,2,1:T(8,128)(2,1)} %get-tuple-element.18) | data formatting | bytes 4194304 | tf_op jit(solution)/shard_map/jit(dynamic_index_in_dim)/dynamic_slice | solution.py:189
  90.6 4.1 %collective-permute-done.5 = f32[512,256]{1,0:T(8,128)} collective-permute-done((f32[512,256]{1,0:T(8,128)S(1)}, f32[512,256]{1,0:T(8,128)}, u32[]{:S(2)}, u32[]{:S(2)}) %collective-permute-start.5) | collective-permute-done | bytes 524320 | tf_op jit(solution)/shard_map/ppermute | solution.py:143
  94.7 2.2 %collective-permute-start.16 = (bf16[512,512]{1,0:T(8,128)(2,1)S(1)}, bf16[512,512]{1,0:T(8,128)(2,1)}, u32[]{:S(2)}, u32[]{:S(2)}) collective-permute-start(bf16[512,512]{1,0:T(8,128)(2,1)S(1)} %get-tuple-element.12), channel_id=1, source_target_pairs={{0,4},{4,0},{8,12},{12,8},{16,20},{20,16},{24,28},{28,24},{1,5},{5... | collective-permute-start | bytes 1572872 | tf_op jit(solution)/shard_map/ppermute | solution.py:147
  100.1 9.5 %collective-permute-start.20 = (bf16[512,256]{1,0:T(8,128)(2,1)S(1)}, bf16[512,256]{1,0:T(8,128)(2,1)S(1)}, u32[]{:S(2)}, u32[]{:S(2)}) collective-permute-start(bf16[512,256]{1,0:T(8,128)(2,1)S(1)} %add_convert_fusion.5), channel_id=1, source_target_pairs={{0,4},{4,0},{8,12},{12,8},{16,20},{20,16},{24,28},{28,24},{1,5},{5... | collective-permute-start | bytes 786440 | tf_op jit(solution)/shard_map/ppermute | solution.py:147
  112.7 1.9 collective-permute-start.11
  114.6 1.8 convolution_convert_fusion.1
  116.4 18.5 %collective-permute-start.19 = (bf16[512,512]{1,0:T(8,128)(2,1)S(1)}, bf16[512,512]{1,0:T(8,128)(2,1)S(1)}, u32[]{:S(2)}, u32[]{:S(2)}) collective-permute-start(bf16[512,512]{1,0:T(8,128)(2,1)S(1)} %convolution_convert_fusion.1), channel_id=1, source_target_pairs={{0,24},{4,28},{8,16},{12,20},{16,8},{20,12},{24,0},{28,4},{1,25},{... | collective-permute-start | bytes 1572872 | tf_op jit(solution)/shard_map/ppermute | solution.py:147
  134.9 1.8 convolution_convert_fusion.2
  141.5 1.8 convolution_convert_fusion.3
  143.3 3.5 %collective-permute-start.17 = (bf16[512,512]{1,0:T(8,128)(2,1)S(1)}, bf16[512,512]{1,0:T(8,128)(2,1)S(1)}, u32[]{:S(2)}, u32[]{:S(2)}) collective-permute-start(bf16[512,512]{1,0:T(8,128)(2,1)S(1)} %convolution_convert_fusion.3), channel_id=1, source_target_pairs={{0,8},{4,12},{8,0},{12,4},{16,24},{20,28},{24,16},{28,20},{1,9},{5... | collective-permute-start | bytes 1572872 | tf_op jit(solution)/shard_map/ppermute | solution.py:147
  146.8 2.9 %collective-permute-start.22 = (bf16[512,256]{1,0:T(8,128)(2,1)S(1)}, bf16[512,256]{1,0:T(8,128)(2,1)S(1)}, u32[]{:S(2)}, u32[]{:S(2)}) collective-permute-start(bf16[512,256]{1,0:T(8,128)(2,1)S(1)} %convolution_convert_fusion.5), channel_id=1, source_target_pairs={{0,16},{4,20},{8,24},{12,28},{16,0},{20,4},{24,8},{28,12},{1,17},{... | collective-permute-start | bytes 786440 | tf_op jit(solution)/shard_map/ppermute | solution.py:147
  149.7 4.4 %collective-permute-done.23 = bf16[512,256]{1,0:T(8,128)(2,1)S(1)} collective-permute-done((bf16[512,256]{1,0:T(8,128)(2,1)S(1)}, bf16[512,256]{1,0:T(8,128)(2,1)S(1)}, u32[]{:S(2)}, u32[]{:S(2)}) %collective-permute-start.23) | collective-permute-done | bytes 262176 | tf_op jit(solution)/shard_map/ppermute | solution.py:147
  154.2 2.0 add_convert_fusion.4
  156.2 13.8 %collective-permute-done.22 = bf16[512,256]{1,0:T(8,128)(2,1)S(1)} collective-permute-done((bf16[512,256]{1,0:T(8,128)(2,1)S(1)}, bf16[512,256]{1,0:T(8,128)(2,1)S(1)}, u32[]{:S(2)}, u32[]{:S(2)}) %collective-permute-start.22) | collective-permute-done | bytes 262176 | tf_op jit(solution)/shard_map/ppermute | solution.py:147
  174.8 2.8 %fusion.1 = f32[512,512]{1,0:T(8,128)} fusion(bf16[1024,512]{1,0:T(8,128)(2,1)S(1)} %constant_dynamic-update-slice_fusion, bf16[512,512]{1,0:T(8,128)(2,1)S(1)} %collective-permute-done.19, bf16[512,512]{1,0:T(8,128)(2,1)S(1)} %collective-permute-done.18, bf16[512,512]{1,0:T(8,128)(2,1)S(1)} %collective-permute-done.17, s32[]{:T(128)S(6)} %select_n.90, ...), kind=kOutput, calls=%fused_computation.15 | convolution fusion | flops 540540928 | bytes 7864324 | tf_op jit(solution)/shard_map/dot_general | solution.py:27
  177.7 1.7 fusion.18
  179.4 2.8 %add_convert_fusion.2 = bf16[512,1024]{1,0:T(8,128)(2,1)} fusion(f32[512,1024]{1,0:T(8,128)S(1)} %fusion.18, bf16[512,512]{1,0:T(8,128)(2,1)} %collective-permute-done.9, bf16[1024,768]{1,0:T(8,128)(2,1)S(1)} %copy-done.12), kind=kOutput, calls=%fused_computation.10 | convolution fusion | flops 537919488 | bytes 4718592 | tf_op jit(solution)/shard_map/dot_general | solution.py:21
  183.7 1.7 fusion.16
  186.3 5.2 %collective-permute-done.12 = bf16[512,512]{1,0:T(8,128)(2,1)} collective-permute-done((bf16[512,512]{1,0:T(8,128)(2,1)}, bf16[512,512]{1,0:T(8,128)(2,1)}, u32[]{:S(2)}, u32[]{:S(2)}) %collective-permute-start.12) | collective-permute-done | bytes 524320 | tf_op jit(solution)/shard_map/ppermute | solution.py:152
  191.5 2.9 %add_convert_fusion = bf16[512,1024]{1,0:T(8,128)(2,1)} fusion(bf16[512,1024]{1,0:T(8,128)(2,1)S(1)} %copy-done.10, bf16[512,1024]{1,0:T(8,128)(2,1)S(1)} %add_convert_fusion.3, bf16[512,1024]{1,0:T(8,128)(2,1)S(1)} %add_convert_fusion.4, f32[512,1024]{1,0:T(8,128)S(1)} %fusion.16, bf16[512,512]{1,0:T(8,128)(2,1)} %collective-permute-done.12, ...), kind=kOutput, calls=%fused_computation.8 | convolution fusion | flops 542113792 | bytes 7864320 | tf_op jit(solution)/shard_map/dot_general | solution.py:21
  (112 shorter events, 36.2 us)
Async XLA Ops:
  7.2 17.5 %copy-start.21 = (bf16[4096,128]{1,0:T(8,128)(2,1)S(1)}, bf16[4096,128]{1,0:T(8,128)(2,1)}, u32[]{:S(2)}) copy-start(bf16[4096,128]{1,0:T(8,128)(2,1)} %param.9) | copy-start | bytes 3145732
  7.2 170.5 %all-gather.6.cloned.1.call-start = ((), (), s32[]{:S(2)}) async-start(), calls=%async_computation.1 | async-start | bytes 1769472 | tf_op jit(solution)/shard_map/all_gather | solution.py:185
  9.9 13.2 %collective-permute-start.10 = (bf16[128,768]{1,0:T(8,128)(2,1)S(1)}, bf16[128,768]{1,0:T(8,128)(2,1)S(1)}, u32[]{:S(2)}, u32[]{:S(2)}) collective-permute-start(bf16[128,768]{1,0:T(8,128)(2,1)S(1)} %pad_maximum_fusion.3), channel_id=1, source_target_pairs={{0,2},{1,3},{2,0},{3,1},{4,6},{5,7},{6,4},{7,5},{8,10},{9,11},{10,... | collective-permute-start | bytes 589832 | tf_op jit(solution)/shard_map/ppermute | solution.py:152
  23.8 158.3 %all-gather.4.cloned.1.call-start = ((), (), s32[]{:S(2)}) async-start(), calls=%async_computation | async-start | bytes 1769472 | tf_op jit(solution)/shard_map/all_gather | solution.py:185
  23.9 8.7 %collective-permute-start.7 = (bf16[128,768]{1,0:T(8,128)(2,1)S(1)}, bf16[128,768]{1,0:T(8,128)(2,1)S(1)}, u32[]{:S(2)}, u32[]{:S(2)}) collective-permute-start(bf16[128,768]{1,0:T(8,128)(2,1)S(1)} %pad_maximum_fusion.2), channel_id=1, source_target_pairs={{0,1},{1,2},{2,3},{3,0},{4,5},{5,6},{6,7},{7,4},{8,9},{9,10},{10,1... | collective-permute-start | bytes 589832 | tf_op jit(solution)/shard_map/ppermute | solution.py:152
  33.3 150.4 %all-gather.8.cloned.1.call-start = ((), (), s32[]{:S(2)}) async-start(), calls=%async_computation.2 | async-start | bytes 1769472 | tf_op jit(solution)/shard_map/all_gather | solution.py:185
  33.4 31.9 %collective-permute-start = (bf16[512,256]{1,0:T(8,128)(2,1)S(1)}, bf16[512,256]{1,0:T(8,128)(2,1)S(1)}, u32[]{:S(2)}, u32[]{:S(2)}) collective-permute-start(bf16[512,256]{1,0:T(8,128)(2,1)S(1)} %pad_maximum_fusion.1.kv0), channel_id=1, source_target_pairs={{0,4},{4,8},{8,12},{12,16},{16,20},{20,24},{24,28},{1,5},{5,9},{9,... | collective-permute-start | bytes 786440 | tf_op jit(solution)/shard_map/ppermute | solution.py:143
  34.7 31.3 %collective-permute-start.1 = (bf16[512,256]{1,0:T(8,128)(2,1)S(1)}, bf16[512,256]{1,0:T(8,128)(2,1)S(1)}, u32[]{:S(2)}, u32[]{:S(2)}) collective-permute-start(bf16[512,256]{1,0:T(8,128)(2,1)S(1)} %pad_maximum_fusion.1.kv0), channel_id=1, source_target_pairs={{0,8},{4,12},{8,16},{12,20},{16,24},{20,28},{1,9},{5,13},{9,17},{1... | collective-permute-start | bytes 786440 | tf_op jit(solution)/shard_map/ppermute | solution.py:143
  38.7 27.9 %collective-permute-start.2 = (bf16[512,256]{1,0:T(8,128)(2,1)S(1)}, bf16[512,256]{1,0:T(8,128)(2,1)S(1)}, u32[]{:S(2)}, u32[]{:S(2)}) collective-permute-start(bf16[512,256]{1,0:T(8,128)(2,1)S(1)} %pad_maximum_fusion.1.kv0), channel_id=1, source_target_pairs={{0,12},{4,16},{8,20},{12,24},{16,28},{1,13},{5,17},{9,21},{13,25},... | collective-permute-start | bytes 786440 | tf_op jit(solution)/shard_map/ppermute | solution.py:143
  58.2 56.4 %collective-permute-start.15 = (bf16[512,4,512]{2,0,1:T(8,128)(2,1)}, bf16[512,4,512]{2,0,1:T(8,128)(2,1)}, u32[]{:S(2)}, u32[]{:S(2)}) collective-permute-start(bf16[512,4,512]{2,0,1:T(8,128)(2,1)} %bitcast.48), channel_id=1, source_target_pairs={{0,4},{4,0},{8,12},{12,8},{16,20},{20,16},{24,28},{28,24},{1,5},{5... | collective-permute-start | bytes 6291464 | tf_op jit(solution)/shard_map/ppermute | solution.py:147
  58.4 9.0 %copy-start = (bf16[512,512]{1,0:T(8,128)(2,1)S(1)}, bf16[512,512]{1,0:T(8,128)(2,1)}, u32[]{:S(2)}) copy-start(bf16[512,512]{1,0:T(8,128)(2,1)} %grad_ref.1) | copy-start | bytes 1572868
  71.3 13.0 %copy-start.19 = (bf16[128,128]{1,0:T(8,128)(2,1)S(1)}, bf16[128,128]{1,0:T(8,128)(2,1)}, u32[]{:S(2)}) copy-start(bf16[128,128]{1,0:T(8,128)(2,1)} %get-tuple-element.25) | copy-start | bytes 98308
  71.3 13.0 %copy-start.20 = (bf16[128,128]{1,0:T(8,128)(2,1)S(1)}, bf16[128,128]{1,0:T(8,128)(2,1)}, u32[]{:S(2)}) copy-start(bf16[128,128]{1,0:T(8,128)(2,1)} %get-tuple-element.32) | copy-start | bytes 98308
  80.4 14.3 %collective-permute-start.5 = (f32[512,256]{1,0:T(8,128)S(1)}, f32[512,256]{1,0:T(8,128)}, u32[]{:S(2)}, u32[]{:S(2)}) collective-permute-start(f32[512,256]{1,0:T(8,128)S(1)} %get-tuple-element.16), channel_id=1, source_target_pairs={{12,0},{16,4},{20,8},{24,12},{28,16},{13,1},{17,5},{21,9},{25,13},... | collective-permute-start | bytes 1572872 | tf_op jit(solution)/shard_map/ppermute | solution.py:143
  81.7 16.9 %collective-permute-start.4 = (f32[512,256]{1,0:T(8,128)S(1)}, f32[512,256]{1,0:T(8,128)}, u32[]{:S(2)}, u32[]{:S(2)}) collective-permute-start(f32[512,256]{1,0:T(8,128)S(1)} %get-tuple-element.15), channel_id=1, source_target_pairs={{8,0},{12,4},{16,8},{20,12},{24,16},{28,20},{9,1},{13,5},{17,9},{2... | collective-permute-start | bytes 1572872 | tf_op jit(solution)/shard_map/ppermute | solution.py:143
  83.0 15.6 %collective-permute-start.3 = (f32[512,256]{1,0:T(8,128)S(1)}, f32[512,256]{1,0:T(8,128)}, u32[]{:S(2)}, u32[]{:S(2)}) collective-permute-start(f32[512,256]{1,0:T(8,128)S(1)} %get-tuple-element.14), channel_id=1, source_target_pairs={{4,0},{8,4},{12,8},{16,12},{20,16},{24,20},{28,24},{5,1},{9,5},{13... | collective-permute-start | bytes 1572872 | tf_op jit(solution)/shard_map/ppermute | solution.py:143
  84.4 6.0 %collective-permute-start.13 = (bf16[128,768]{1,0:T(8,128)(2,1)S(1)}, bf16[128,768]{1,0:T(8,128)(2,1)S(1)}, u32[]{:S(2)}, u32[]{:S(2)}) collective-permute-start(bf16[128,768]{1,0:T(8,128)(2,1)S(1)} %pad_maximum_fusion.4), channel_id=1, source_target_pairs={{0,3},{1,0},{2,1},{3,2},{4,7},{5,4},{6,5},{7,6},{8,11},{9,8},{10,9... | collective-permute-start | bytes 589832 | tf_op jit(solution)/shard_map/ppermute | solution.py:152
  90.3 19.3 %collective-permute-start.6 = (bf16[512,512]{1,0:T(8,128)(2,1)S(1)}, bf16[512,512]{1,0:T(8,128)(2,1)S(1)}, u32[]{:S(2)}, u32[]{:S(2)}) collective-permute-start(bf16[512,512]{1,0:T(8,128)(2,1)S(1)} %get-tuple-element.12), channel_id=1, source_target_pairs={{0,1},{1,2},{2,3},{3,0},{4,5},{5,6},{6,7},{7,4},{8,9},{9,10},{10,1... | collective-permute-start | bytes 1572872 | tf_op jit(solution)/shard_map/ppermute | solution.py:152
  94.7 16.5 %collective-permute-start.16 = (bf16[512,512]{1,0:T(8,128)(2,1)S(1)}, bf16[512,512]{1,0:T(8,128)(2,1)}, u32[]{:S(2)}, u32[]{:S(2)}) collective-permute-start(bf16[512,512]{1,0:T(8,128)(2,1)S(1)} %get-tuple-element.12), channel_id=1, source_target_pairs={{0,4},{4,0},{8,12},{12,8},{16,20},{20,16},{24,28},{28,24},{1,5},{5... | collective-permute-start | bytes 1572872 | tf_op jit(solution)/shard_map/ppermute | solution.py:147
  100.0 14.6 %copy-start.8 = (bf16[512,4,1,512]{3,0,2,1:T(8,128)(2,1)S(1)}, bf16[512,4,1,512]{3,0,2,1:T(8,128)(2,1)}, u32[]{:S(2)}) copy-start(bf16[512,4,1,512]{3,0,2,1:T(8,128)(2,1)} %copy.23) | copy-start | bytes 6291460
  100.0 12.7 %collective-permute-start.8 = (bf16[512,256]{1,0:T(8,128)(2,1)S(1)}, bf16[512,256]{1,0:T(8,128)(2,1)S(1)}, u32[]{:S(2)}, u32[]{:S(2)}) collective-permute-start(bf16[512,256]{1,0:T(8,128)(2,1)S(1)} %add_convert_fusion.5), channel_id=1, source_target_pairs={{0,1},{1,2},{2,3},{3,0},{4,5},{5,6},{6,7},{7,4},{8,9},{9,10},{10,1... | collective-permute-start | bytes 786440 | tf_op jit(solution)/shard_map/ppermute | solution.py:152
  100.1 36.7 %collective-permute-start.20 = (bf16[512,256]{1,0:T(8,128)(2,1)S(1)}, bf16[512,256]{1,0:T(8,128)(2,1)S(1)}, u32[]{:S(2)}, u32[]{:S(2)}) collective-permute-start(bf16[512,256]{1,0:T(8,128)(2,1)S(1)} %add_convert_fusion.5), channel_id=1, source_target_pairs={{0,4},{4,0},{8,12},{12,8},{16,20},{20,16},{24,28},{28,24},{1,5},{5... | collective-permute-start | bytes 786440 | tf_op jit(solution)/shard_map/ppermute | solution.py:147
  109.7 37.1 %collective-permute-start.9 = (bf16[512,512]{1,0:T(8,128)(2,1)S(1)}, bf16[512,512]{1,0:T(8,128)(2,1)}, u32[]{:S(2)}, u32[]{:S(2)}) collective-permute-start(bf16[512,512]{1,0:T(8,128)(2,1)S(1)} %collective-permute-done.6), channel_id=1, source_target_pairs={{0,1},{1,2},{2,3},{3,0},{4,5},{5,6},{6,7},{7,4},{8,9},{9,10},{10,1... | collective-permute-start | bytes 1572872 | tf_op jit(solution)/shard_map/ppermute | solution.py:152
  112.7 30.6 %collective-permute-start.11 = (bf16[512,256]{1,0:T(8,128)(2,1)S(1)}, bf16[512,256]{1,0:T(8,128)(2,1)}, u32[]{:S(2)}, u32[]{:S(2)}) collective-permute-start(bf16[512,256]{1,0:T(8,128)(2,1)S(1)} %collective-permute-done.8), channel_id=1, source_target_pairs={{0,1},{1,2},{2,3},{3,0},{4,5},{5,6},{6,7},{7,4},{8,9},{9,10},{10,1... | collective-permute-start | bytes 786440 | tf_op jit(solution)/shard_map/ppermute | solution.py:152
  116.4 58.4 %collective-permute-start.19 = (bf16[512,512]{1,0:T(8,128)(2,1)S(1)}, bf16[512,512]{1,0:T(8,128)(2,1)S(1)}, u32[]{:S(2)}, u32[]{:S(2)}) collective-permute-start(bf16[512,512]{1,0:T(8,128)(2,1)S(1)} %convolution_convert_fusion.1), channel_id=1, source_target_pairs={{0,24},{4,28},{8,16},{12,20},{16,8},{20,12},{24,0},{28,4},{1,25},{... | collective-permute-start | bytes 1572872 | tf_op jit(solution)/shard_map/ppermute | solution.py:147
  136.7 38.1 %collective-permute-start.18 = (bf16[512,512]{1,0:T(8,128)(2,1)S(1)}, bf16[512,512]{1,0:T(8,128)(2,1)S(1)}, u32[]{:S(2)}, u32[]{:S(2)}) collective-permute-start(bf16[512,512]{1,0:T(8,128)(2,1)S(1)} %convolution_convert_fusion.2), channel_id=1, source_target_pairs={{0,16},{4,20},{8,24},{12,28},{16,0},{20,4},{24,8},{28,12},{1,17},{... | collective-permute-start | bytes 1572872 | tf_op jit(solution)/shard_map/ppermute | solution.py:147
  138.3 15.9 %collective-permute-start.23 = (bf16[512,256]{1,0:T(8,128)(2,1)S(1)}, bf16[512,256]{1,0:T(8,128)(2,1)S(1)}, u32[]{:S(2)}, u32[]{:S(2)}) collective-permute-start(bf16[512,256]{1,0:T(8,128)(2,1)S(1)} %convolution_convert_fusion.4), channel_id=1, source_target_pairs={{0,24},{4,28},{8,16},{12,20},{16,8},{20,12},{24,0},{28,4},{1,25},{... | collective-permute-start | bytes 786440 | tf_op jit(solution)/shard_map/ppermute | solution.py:147
  143.3 31.5 %collective-permute-start.17 = (bf16[512,512]{1,0:T(8,128)(2,1)S(1)}, bf16[512,512]{1,0:T(8,128)(2,1)S(1)}, u32[]{:S(2)}, u32[]{:S(2)}) collective-permute-start(bf16[512,512]{1,0:T(8,128)(2,1)S(1)} %convolution_convert_fusion.3), channel_id=1, source_target_pairs={{0,8},{4,12},{8,0},{12,4},{16,24},{20,28},{24,16},{28,20},{1,9},{5... | collective-permute-start | bytes 1572872 | tf_op jit(solution)/shard_map/ppermute | solution.py:147
  146.8 23.2 %collective-permute-start.22 = (bf16[512,256]{1,0:T(8,128)(2,1)S(1)}, bf16[512,256]{1,0:T(8,128)(2,1)S(1)}, u32[]{:S(2)}, u32[]{:S(2)}) collective-permute-start(bf16[512,256]{1,0:T(8,128)(2,1)S(1)} %convolution_convert_fusion.5), channel_id=1, source_target_pairs={{0,16},{4,20},{8,24},{12,28},{16,0},{20,4},{24,8},{28,12},{1,17},{... | collective-permute-start | bytes 786440 | tf_op jit(solution)/shard_map/ppermute | solution.py:147
  154.2 16.7 %collective-permute-start.21 = (bf16[512,256]{1,0:T(8,128)(2,1)S(1)}, bf16[512,256]{1,0:T(8,128)(2,1)S(1)}, u32[]{:S(2)}, u32[]{:S(2)}) collective-permute-start(bf16[512,256]{1,0:T(8,128)(2,1)S(1)} %convolution_convert_fusion.6), channel_id=1, source_target_pairs={{0,8},{4,12},{8,0},{12,4},{16,24},{20,28},{24,16},{28,20},{1,9},{5... | collective-permute-start | bytes 786440 | tf_op jit(solution)/shard_map/ppermute | solution.py:147
  170.0 13.7 %collective-permute-start.14 = (bf16[512,256]{1,0:T(8,128)(2,1)}, bf16[512,256]{1,0:T(8,128)(2,1)}, u32[]{:S(2)}, u32[]{:S(2)}) collective-permute-start(bf16[512,256]{1,0:T(8,128)(2,1)} %collective-permute-done.11), channel_id=1, source_target_pairs={{0,1},{1,2},{2,3},{3,0},{4,5},{5,6},{6,7},{7,4},{8,9},{9,10},{10,1... | collective-permute-start | bytes 786440 | tf_op jit(solution)/shard_map/ppermute | solution.py:152
  170.9 20.6 %collective-permute-start.12 = (bf16[512,512]{1,0:T(8,128)(2,1)}, bf16[512,512]{1,0:T(8,128)(2,1)}, u32[]{:S(2)}, u32[]{:S(2)}) collective-permute-start(bf16[512,512]{1,0:T(8,128)(2,1)} %collective-permute-done.9), channel_id=1, source_target_pairs={{0,1},{1,2},{2,3},{3,0},{4,5},{5,6},{6,7},{7,4},{8,9},{9,10},{10,1... | collective-permute-start | bytes 1572872 | tf_op jit(solution)/shard_map/ppermute | solution.py:152
  (19 other events, 52.4 us)
Sparse Core Ops, SparseCore 0:
  24.0 31.9 all-gather.5
  57.8 28.2 all-gather.3
  98.1 51.5 all-gather.7
where the time goes:
time: 202 us; the launch traced here: 201 us
  starting transfers between devices  63.3 us (31%)
  waiting for transfers between devices  40.2 us (20%)
  matrix products  39.8 us (20%)
  local copies, waits for them, and re-layouts  32.4 us (16%)
  between operations  14.2 us (7%)
  Pallas kernels  9.12 us (5%)
    ppermute x9, starting transfers between devices, swap(): lax.ppermute(value, axis, [(i, i ^ mask) for i in range(lax.axis_size(axi...  36.8 us
    ppermute x9, waiting for transfers between devices, swap(): lax.ppermute(value, axis, [(i, i ^ mask) for i in range(lax.axis_size(axi...  18.3 us
    ppermute x9, waiting for transfers between devices, rotate(): lax.ppermute(value, axis, [(i, (i + steps) % count) for i in range(count)])  17.1 us
    dot_general x8, matrix products, dot_tn(): lax.dot_general(left_mat, right_mat, (((0,), (0,)), ((), ())), preferred_...  14.3 us
    unnamed x50, local copies, waits for them, and re-layouts  13.9 us
    dot_general x8, matrix products, dot_nt(): lax.dot_general(left_mat, right_mat, (((1,), (1,)), ((), ())), preferred_...  13.8 us
    ppermute x6, starting transfers between devices, shift(): return lax.ppermute(value, axis, pairs)  13.5 us
    ppermute x9, starting transfers between devices, rotate(): lax.ppermute(value, axis, [(i, (i + steps) % count) for i in range(count)])  12.8 us
  transfers between devices with their start and end apart: 27, of which 7 were waited for; matrix products, arithmetic and copies ran while one was open for 30% of the time, Pallas kernels for 5%

commit v1 on v0

--- a/solution.py
+++ b/solution.py
@@ -12,6 +12,8 @@
 SPAN = 3
 GRAIN = 128
 TILE = 256
+CHUNK = 512
+MIB = 2**20
 
 NEG = -1e30
 LOG2E = 1.4426950408889634
@@ -33,15 +35,243 @@
     return jnp.dot(left_mat, right_mat, preferred_element_type=jnp.float32)
 
 
+def in_hbm(*arrays):
+    return [pltpu.with_memory_space_constraint(array, pltpu.HBM) for array in arrays]
+
+
+def project_kernel(place_ref, x_ref, wq_ref, wk_ref, wv_ref, q_ref, kv_ref, *refs):
+    piece_refs, acc_ref = refs[:-1], refs[-1]
+    step = pl.program_id(0)
+    at = 0
+    for weight_ref in (wq_ref, wk_ref, wv_ref):
+        cols = slice(at, at + weight_ref.shape[1])
+        at = cols.stop
+        term = dot_nn(x_ref[...], weight_ref[...])
+
+        @pl.when(step == 0)
+        def _():
+            acc_ref[:, cols] = term
+
+        @pl.when(step > 0)
+        def _():
+            acc_ref[:, cols] += term
+
+    n_head = len(piece_refs) + 1
+    per_head = pl.num_programs(0) // n_head
+    piece = piece_refs[0].shape[0]
+    chunk = x_ref.shape[1]
+    group = step // per_head
+    first = place_ref[1] - step % per_head * chunk
+    here = (first >= 0) & (first < chunk)
+    for distance, piece_ref in enumerate(piece_refs, 1):
+
+        @pl.when(here & (group == (place_ref[0] + distance) % n_head))
+        def _():
+            rows = pl.ds(pl.multiple_of(first, piece), piece)
+            at = 0
+            for weight_ref in (wq_ref, wk_ref, wv_ref):
+                cols = slice(at, at + weight_ref.shape[1])
+                at = cols.stop
+                piece_ref[:, cols] = weight_ref[rows, :]
+
+    @pl.when(step == pl.num_programs(0) - 1)
+    def _():
+        q_cols = q_ref.shape[1]
+        q_ref[...] = acc_ref[:, :q_cols].astype(q_ref.dtype)
+        kv_ref[...] = acc_ref[:, q_cols:].astype(kv_ref.dtype)
+
+
+def project(place, inputs, weights, n_head, piece):
+    rows, width = inputs.shape
+    widths = [weight.shape[1] for weight in weights]
+    cols = sum(widths)
+
+    def fixed(shape):
+        return pl.BlockSpec(shape, lambda i, place: (0, 0))
+
+    shapes = [(rows, widths[0]), (rows, cols - widths[0])] + [(piece, cols)] * (n_head - 1)
+    return pl.pallas_call(
+        project_kernel,
+        grid_spec=pltpu.PrefetchScalarGridSpec(
+            num_scalar_prefetch=1,
+            grid=(width // CHUNK,),
+            in_specs=[pl.BlockSpec((rows, CHUNK), lambda i, place: (0, i))]
+            + [pl.BlockSpec((CHUNK, cols), lambda i, place: (i, 0)) for cols in widths],
+            out_specs=tuple(fixed(shape) for shape in shapes),
+            scratch_shapes=[pltpu.VMEM((rows, cols), jnp.float32)],
+        ),
+        out_shape=tuple(jax.ShapeDtypeStruct(shape, jnp.bfloat16) for shape in shapes),
+        compiler_params=pltpu.CompilerParams(vmem_limit_bytes=32 * MIB),
+        cost_estimate=pl.CostEstimate(
+            flops=2 * rows * width * cols, bytes_accessed=2 * width * (rows + cols), transcendentals=0
+        ),
+        name="project",
+    )(place, *in_hbm(inputs, *weights))
+
+
+def combine_kernel(own_ref, *refs):
+    back_refs, (dq_ref, dq_t_ref, low_ref, joined_ref, turned_ref) = refs[:-5], refs[-5:]
+    total = own_ref[...]
+    for back_ref in back_refs:
+        total = total + back_ref[...].astype(jnp.float32)
+    low = total.astype(jnp.bfloat16)
+    q_cols = dq_ref.shape[1]
+    low_ref[...] = low
+    joined_ref[:, :q_cols] = dq_ref[...]
+    joined_ref[:, q_cols:] = low
+    turned_ref[:q_cols, :] = dq_t_ref[...]
+    turned_ref[q_cols:, :] = total.T.astype(jnp.bfloat16)
+
+
+def combine(own, back, dq, dq_turned):
+    rows, cols = own.shape
+    wide = dq.shape[1] + cols
+    vmem = pl.BlockSpec(memory_space=pltpu.VMEM)
+    shapes = ((rows, cols), (rows, wide), (wide, rows))
+    return pl.pallas_call(
+        combine_kernel,
+        out_shape=tuple(jax.ShapeDtypeStruct(shape, jnp.bfloat16) for shape in shapes),
+        in_specs=[vmem] * (len(back) + 3),
+        out_specs=(vmem,) * 3,
+        compiler_params=pltpu.CompilerParams(vmem_limit_bytes=16 * MIB),
+        cost_estimate=pl.CostEstimate(flops=rows * cols * 4, bytes_accessed=4 * MIB, transcendentals=0),
+        name="combine",
+    )(own, *back, dq, dq_turned)
+
+
+def terms_kernel(index_ref, joined_ref, other_joined_ref, x_ref, other_x_ref, *out_refs):
+    step = pl.program_id(0)
+    term = dot_nn(joined_ref[...], x_ref[...]) + dot_nn(other_joined_ref[...], other_x_ref[...])
+    for chip, out_ref in enumerate(out_refs):
+
+        @pl.when(step == chip)
+        def _():
+            out_ref[...] = term.astype(out_ref.dtype)
+
+
+def weight_terms(index, joined, other_joined, inputs, other_inputs, n_ctx):
+    cols, rows = joined.shape
+    kept = inputs.shape[1] // n_ctx
+    chips = n_ctx // 2
+    whole = pl.BlockSpec((cols, rows), lambda i, index: (0, 0))
+    part = pl.BlockSpec((rows, kept), lambda i, index: (0, index[i]))
+    return pl.pallas_call(
+        terms_kernel,
+        grid_spec=pltpu.PrefetchScalarGridSpec(
+            num_scalar_prefetch=1,
+            grid=(chips,),
+            in_specs=[whole, whole, part, part],
+            out_specs=(pl.BlockSpec((cols, kept), lambda i, index: (0, 0)),) * chips,
+        ),
+        out_shape=tuple(
+            jax.ShapeDtypeStruct((cols, kept), jnp.float32 if chip == 0 else jnp.bfloat16)
+            for chip in range(chips)
+        ),
+        compiler_params=pltpu.CompilerParams(vmem_limit_bytes=32 * MIB),
+        cost_estimate=pl.CostEstimate(
+            flops=4 * cols * rows * kept * chips, bytes_accessed=10 * MIB, transcendentals=0
+        ),
+        name="weight_terms",
+    )(index, joined, other_joined, inputs, other_inputs)
+
+
+def rows_kernel(*refs):
+    in_refs, out_refs = refs[:-3], refs[-3:]
+    total = in_refs[0][...]
+    for in_ref in in_refs[1:]:
+        total = total + in_ref[...].astype(jnp.float32)
+    at = 0
+    for out_ref in out_refs:
+        cols = slice(at, at + out_ref.shape[1])
+        at = cols.stop
+        out_ref[...] = total[cols, :].T
+
+
+def weight_rows(terms, widths):
+    kept = terms[0].shape[1]
+    vmem = pl.BlockSpec(memory_space=pltpu.VMEM)
+    return pl.pallas_call(
+        rows_kernel,
+        out_shape=tuple(jax.ShapeDtypeStruct((kept, width), jnp.float32) for width in widths),
+        in_specs=[vmem] * len(terms),
+        out_specs=(vmem,) * 3,
+        compiler_params=pltpu.CompilerParams(vmem_limit_bytes=32 * MIB),
+        cost_estimate=pl.CostEstimate(flops=4 * MIB, bytes_accessed=6 * MIB, transcendentals=0),
+        name="weight_rows",
+    )(*terms)
+
+
+def products_kernel(firsts, has_base, *refs):
+    refs = refs[1:]
+    out_ref = refs[-1]
+    n_terms = len(firsts)
+    total = refs[2 * n_terms][...] if has_base else None
+    for at, first in enumerate(firsts):
+        rows = refs[n_terms + at][...]
+        rows = rows.reshape(-1, rows.shape[-1])
+        term = dot_nt(refs[at][:, first : first + rows.shape[1]], rows)
+        total = term if total is None else total + term
+    out_ref[...] = total.astype(out_ref.dtype)
+
+
+def products(lefts, rights, base, out_width, head, dtype, name):
+    rows = lefts[0].shape[0]
+    block = 256
+    n_blocks = out_width // block
+    left_specs = [pl.BlockSpec(left.shape, lambda i, head: (0, 0)) for left in lefts]
+    right_specs = []
+    firsts = []
+    flops = 0
+    for left, (array, *place) in zip(lefts, rights):
+        cols = array.shape[1] if len(place) == 1 else place[2]
+        flops += 2 * rows * cols * out_width
+        if len(place) == 1:
+            firsts.append(place[0])
+            right_specs.append(
+                pl.BlockSpec((block, cols), lambda i, head: (head[0] * n_blocks + i, 0))
+            )
+        else:
+            step, first, cols = place
+            piece = array.shape[2]
+            firsts.append(0)
+            right_specs.append(
+                pl.BlockSpec(
+                    (block // piece, 1, piece, cols),
+                    partial(lambda step, at, i, head: (i, step, 0, at), step, first // cols),
+                )
+            )
+    out_spec = pl.BlockSpec((rows, block), lambda i, head: (0, i))
+    extra = [] if base is None else [base]
+    return pl.pallas_call(
+        partial(products_kernel, tuple(firsts), base is not None),
+        grid_spec=pltpu.PrefetchScalarGridSpec(
+            num_scalar_prefetch=1,
+            grid=(n_blocks,),
+            in_specs=left_specs + right_specs + [out_spec] * len(extra),
+            out_specs=out_spec,
+        ),
+        out_shape=jax.ShapeDtypeStruct((rows, out_width), dtype),
+        compiler_params=pltpu.CompilerParams(vmem_limit_bytes=32 * MIB),
+        cost_estimate=pl.CostEstimate(flops=flops, bytes_accessed=8 * MIB, transcendentals=0),
+        name=name,
+    )(head, *lefts, *in_hbm(*[array for array, *place in rights]), *extra)
+
+
 def attention_kernel(
     first_ref, query_ref, grad_ref, kv0, kv1, kv2, kv3,
-    out_ref, dq_ref, d0, d1, d2, d3,
-    kv_ref, acc_ref, score_ref,
+    out_ref, dq_ref, dq_t_ref, d0, d1, d2, d3,
+    kv_ref, acc_ref, score_ref, sems,
 ):
     rows = query_ref.shape[0]
-    for slot, block in enumerate((kv3, kv2, kv1, kv0)):
-        kv_ref[pl.ds(slot * rows, rows), :] = block[...]
+    copies = [
+        pltpu.make_async_copy(block, kv_ref.at[pl.ds(slot * rows, rows), :], sems.at[slot])
+        for slot, block in enumerate((kv3, kv2, kv1, kv0))
+    ]
+    for copy in copies:
+        copy.start()
     acc_ref[...] = jnp.zeros_like(acc_ref)
+    for copy in copies:
+        copy.wait()
     factor = HD ** (-0.5)
     wide = GROUP * GRAIN
     for granule in range(rows // GRAIN):
@@ -102,36 +332,42 @@
             return accum + dot_tn(kv_ref[tile_rows(tile), :HD], dscore)
 
         accum = lax.fori_loop(low, last + 1, grad_tile, jnp.zeros((HD, wide), jnp.float32))
-        dquery = (accum * factor).T.astype(jnp.bfloat16)
+        accum = accum * factor
+        dquery = accum.T.astype(jnp.bfloat16)
         for head, cols in enumerate(heads):
             part = slice(head * GRAIN, (head + 1) * GRAIN)
             out_ref[here, cols] = out[part]
             dq_ref[here, cols] = dquery[part]
+            dq_t_ref[cols, here] = accum[:, part].astype(jnp.bfloat16)
     for slot, block in enumerate((d3, d2, d1, d0)):
         place = pl.ds(slot * rows, rows)
-        block[:, :HD] = acc_ref[place, :HD] * factor
-        block[:, HD:] = acc_ref[place, HD:]
+        block[:, :HD] = (acc_ref[place, :HD] * factor).astype(block.dtype)
+        block[:, HD:] = acc_ref[place, HD:].astype(block.dtype)
 
 
 def attention(first, query, grad, kv_list):
     rows, cols = query.shape
     window = (SPAN + 1) * rows
     low = jax.ShapeDtypeStruct((rows, cols), jnp.bfloat16)
-    high = jax.ShapeDtypeStruct((rows, 2 * HD), jnp.float32)
+    turned = jax.ShapeDtypeStruct((cols, rows), jnp.bfloat16)
+    own = jax.ShapeDtypeStruct((rows, 2 * HD), jnp.float32)
+    sent = jax.ShapeDtypeStruct((rows, 2 * HD), jnp.bfloat16)
     vmem = pl.BlockSpec(memory_space=pltpu.VMEM)
+    anywhere = pl.BlockSpec(memory_space=pl.ANY)
     return pl.pallas_call(
         attention_kernel,
-        out_shape=(low, low) + (high,) * (SPAN + 1),
-        in_specs=[pl.BlockSpec(memory_space=pltpu.SMEM)] + [vmem] * (SPAN + 3),
-        out_specs=(vmem,) * (SPAN + 3),
+        out_shape=(low, low, turned, own) + (sent,) * SPAN,
+        in_specs=[pl.BlockSpec(memory_space=pltpu.SMEM), vmem, vmem] + [anywhere] * (SPAN + 1),
+        out_specs=(vmem,) * (SPAN + 4),
         scratch_shapes=[
             pltpu.VMEM((window, 2 * HD), jnp.bfloat16),
             pltpu.VMEM((window, 2 * HD), jnp.float32),
             pltpu.VMEM((window, GROUP * GRAIN), jnp.float32),
+            pltpu.SemaphoreType.DMA((SPAN + 1,)),
         ],
-        compiler_params=pltpu.CompilerParams(vmem_limit_bytes=32 * 1024 * 1024),
+        compiler_params=pltpu.CompilerParams(vmem_limit_bytes=32 * MIB),
         cost_estimate=pl.CostEstimate(
-            flops=6 * 2 * rows * window * cols, bytes_accessed=6 * 2**20, transcendentals=0
+            flops=6 * 2 * rows * window * cols, bytes_accessed=6 * MIB, transcendentals=0
         ),
         name="attention",
     )(first, query, grad, *kv_list)
@@ -161,34 +397,20 @@
     head = lax.axis_index("head")
     q_cols = query_weight.shape[1]
     k_cols = key_weight.shape[1]
+
     weights = (query_weight, key_weight, value_weight)
-
-    kv_loc = jnp.concatenate(
-        [dot_nn(inputs, key_weight).astype(jnp.bfloat16), dot_nn(inputs, value_weight).astype(jnp.bfloat16)],
-        axis=1,
-    )
-    kv_list = [kv_loc] + [shift(kv_loc, "ctx", distance) for distance in range(1, SPAN + 1)]
-    query = dot_nn(inputs, query_weight).astype(jnp.bfloat16)
-
     out_width = width // n_head
     piece = out_width // n_ctx
-    weight_rows = []
-    for step in range(n_head):
-        if step == 0:
-            start = head * out_width
-            rows = [lax.dynamic_slice_in_dim(w, start, out_width, 0) for w in weights]
-            weight_rows.append(jnp.concatenate(rows, axis=1))
-            continue
-        start = (head + step) % n_head * out_width + ctx * piece
-        rows = [lax.dynamic_slice_in_dim(w, start, piece, 0) for w in weights]
-        moved = rotate(jnp.concatenate(rows, axis=1), "head", step)
-        weight_rows.append(lax.all_gather(moved, "ctx", axis=0, tiled=True))
-
-    split = inputs.reshape(tok_rows, chips, 2, width // n_ctx)
-    core = ctx % 2
-    own_part = lax.dynamic_index_in_dim(split, core, 2, keepdims=False)
-    other_part = lax.dynamic_index_in_dim(split, 1 - core, 2, keepdims=False)
-    pair_inputs = jnp.concatenate([own_part, swap(other_part, "ctx", 1)], axis=0)
+    place = jnp.stack([head, ctx * piece]).astype(jnp.int32)
+    query, kv_loc, *pieces = project(place, inputs, weights, n_head, piece)
+
+    kv_list = [kv_loc] + [shift(kv_loc, "ctx", distance) for distance in range(1, SPAN + 1)]
+    pieces = [rotate(rows, "head", step) for step, rows in enumerate(pieces, 1)]
+    query, kv_list, pieces, inputs = lax.optimization_barrier((query, kv_list, pieces, inputs))
+    gathered = lax.all_gather(jnp.concatenate(pieces, axis=0), "ctx", axis=0, tiled=True)
+    gathered = gathered.reshape(n_ctx, n_head - 1, piece, q_cols + 2 * k_cols)
+
+    other_inputs = swap(inputs, "ctx", 1)
 
     granules = tok_rows // GRAIN
     window_start = (ctx - SPAN) * tok_rows
@@ -197,35 +419,41 @@
     starts = jnp.sum(
         jnp.where(doc_ends[None, :] <= positions[:, None], doc_lengths[None, :], 0), axis=1
     )
-    attn_out, dq_low, *kv_grads = attention(starts - window_start, query, out_grad, kv_list)
-
-    kv_total = kv_grads[0]
-    for distance in range(1, SPAN + 1):
-        kv_total = kv_total + shift(kv_grads[distance], "ctx", -distance)
-    dkv_low = kv_total.astype(jnp.bfloat16)
-
-    grad_sum = jnp.zeros((tok_rows, out_width), jnp.float32)
-    moving = (dq_low, dkv_low)
-    for step in range(n_head):
-        if step > 0:
-            moving = tuple(rotate(part, "head", 1) for part in moving)
-        rows = weight_rows[step]
-        term = dot_nt(moving[0], rows[:, :q_cols]) + dot_nt(moving[1], rows[:, q_cols:])
-        grad_sum = grad_sum + term.astype(jnp.bfloat16).astype(jnp.float32)
-    input_grad = grad_sum.astype(jnp.bfloat16)
-
-    sums = []
-    for low in (dq_low, dkv_low):
-        pair = jnp.concatenate([low, swap(low, "ctx", 1)], axis=0)
-        total = None
-        for chip in range(chips):
-            block = lax.dynamic_index_in_dim(pair_inputs, (ctx // 2) ^ chip, 1, keepdims=False)
-            term = dot_tn(block, pair)
-            if chip > 0:
-                term = swap(term.astype(jnp.bfloat16), "ctx", 2 * chip).astype(jnp.float32)
-            total = term if total is None else total + term
-        sums.append(total)
-    return (attn_out, input_grad, sums[0], sums[1][:, :k_cols], sums[1][:, k_cols:])
+    attn_out, dq_low, dq_turned, own_grads, *sent_grads = attention(
+        starts - window_start, query, out_grad, kv_list
+    )
+
+    dq_up = rotate(dq_low, "head", 1)
+    back = [shift(sent_grads[distance - 1], "ctx", -distance) for distance in range(1, SPAN + 1)]
+    back, dq_up, dq_low, dq_turned = lax.optimization_barrier((back, dq_up, dq_low, dq_turned))
+    dkv_low, joined, turned = combine(own_grads, back, dq_low, dq_turned)
+    joined_down = rotate(joined, "head", -1)
+    dkv_up = rotate(dkv_low, "head", 1)
+
+    other_turned = swap(turned, "ctx", 1)
+    index = ((ctx // 2) ^ jnp.arange(chips, dtype=jnp.int32)) * 2 + ctx % 2
+    terms = weight_terms(index, turned, other_turned, inputs, other_inputs, n_ctx)
+    moved = [swap(term, "ctx", 2 * chip) for chip, term in enumerate(terms) if chip > 0]
+    dq_far = rotate(dq_up, "head", 1)
+    dkv_far = rotate(dkv_up, "head", 1)
+
+    head_index = jnp.reshape(head, (1,)).astype(jnp.int32)
+    q_place, kv_place, place = (0, q_cols), (q_cols, 2 * k_cols), (0, q_cols + 2 * k_cols)
+    dq_up, dkv_up, joined_down, terms = lax.optimization_barrier((dq_up, dkv_up, joined_down, terms))
+    grad_sum = products(
+        (joined, joined, joined, dq_up, dkv_up, joined_down),
+        (
+            (query_weight, 0), (key_weight, q_cols), (value_weight, q_cols + k_cols),
+            (gathered, 0, *q_place), (gathered, 0, *kv_place), (gathered, 2, *place),
+        ),
+        None, out_width, head_index, jnp.float32, "products_near",
+    )
+    input_grad = products(
+        (dq_far, dkv_far), ((gathered, 1, *q_place), (gathered, 1, *kv_place)),
+        grad_sum, out_width, head_index, jnp.bfloat16, "products_far",
+    )
+    weight_grads = weight_rows([terms[0], *moved], (q_cols, k_cols, k_cols))
+    return (attn_out, input_grad, *weight_grads)
 
 
 def solution(mesh):

time: 202 us -> 167 us (0.83)
  matrix products: 39.8 us -> 0 us
  waiting for transfers between devices: 40.2 us -> 71.3 us
  local copies, waits for them, and re-layouts: 32.4 us -> 2.23 us
  Pallas kernels: 9.12 us -> 38.5 us
  starting transfers between devices: 63.3 us -> 40.3 us
    dot_general x19 -> x0, matrix products: 39.8 us -> none  [the longest x8 14.3 us: dot_tn(): lax.dot_general(left_mat, right_mat, (((0,), (0,)), ((), ())), preferred_...]
    pallas_call x1 -> x7, Pallas kernels: 9.12 us -> 38.5 us  [the longest x1 13.8 us: project(): pl.pallas_call(project_kernel, grid_spec=pltpu.PrefetchScalarGridSpec(num...]
    ppermute x6, waiting for transfers between devices: 4.63 us -> 28.9 us  [shift(): return lax.ppermute(value, axis, pairs)]
    ppermute x9 -> x5, starting transfers between devices: 36.8 us -> 12.8 us  [swap(): lax.ppermute(value, axis, [(i, i ^ mask) for i in range(lax.axis_size(axi...]
    dynamic_slice x6 -> x0, local copies, waits for them, and re-layouts: 16.5 us -> none  [the longest x2 8.68 us: body(): other_part = lax.dynamic_index_in_dim(split, 1 - core, 2, keepdims=False)]
    unnamed x50 -> x6, local copies, waits for them, and re-layouts: 13.9 us -> 2.23 us
    ppermute x9 -> x5, waiting for transfers between devices: 18.3 us -> 24.2 us  [swap(): lax.ppermute(value, axis, [(i, i ^ mask) for i in range(lax.axis_size(axi...]
    ppermute x9 -> x8, starting transfers between devices: 12.8 us -> 14 us  [rotate(): lax.ppermute(value, axis, [(i, (i + steps) % count) for i in range(count)])]
  transfers between devices with their start and end apart: 27 -> 20, of which waited for: 7 -> 8; matrix products, arithmetic and copies ran while one was open for 30% -> 0% of each run, Pallas kernels for 5% -> 12%
where the time goes in v1:
time: 167 us; the launch traced here: 168 us
  waiting for transfers between devices  71.3 us (43%)
  starting transfers between devices  40.3 us (24%)
  Pallas kernels  38.5 us (23%)
  between operations  14.2 us (9%)
  local copies, waits for them, and re-layouts  2.23 us (1%)
    ppermute x6, waiting for transfers between devices, shift(): return lax.ppermute(value, axis, pairs)  28.9 us
    ppermute x5, waiting for transfers between devices, swap(): lax.ppermute(value, axis, [(i, i ^ mask) for i in range(lax.axis_size(axi...  24.2 us
    ppermute x8, waiting for transfers between devices, rotate(): lax.ppermute(value, axis, [(i, (i + steps) % count) for i in range(count)])  18.1 us
    ppermute x8, starting transfers between devices, rotate(): lax.ppermute(value, axis, [(i, (i + steps) % count) for i in range(count)])  14 us
    pallas_call x1, Pallas kernels, project(): pl.pallas_call(project_kernel, grid_spec=pltpu.PrefetchScalarGridSpec(num...  13.8 us
    ppermute x6, starting transfers between devices, shift(): return lax.ppermute(value, axis, pairs)  13.5 us
    ppermute x5, starting transfers between devices, swap(): lax.ppermute(value, axis, [(i, i ^ mask) for i in range(lax.axis_size(axi...  12.8 us
    pallas_call x2, Pallas kernels, products(): pl.pallas_call(partial(products_kernel, tuple(firsts), base is not None),...  9.57 us
  transfers between devices with their start and end apart: 20, of which 8 were waited for; matrix products, arithmetic and copies ran while one was open for 0% of the time, Pallas kernels for 12%

profile of v1, /device:TPU:0, one launch (start us, length us, event | category | flops | bytes accessed | tf_op | source)
XLA Modules:
  0.0 167.9 jit_solution(10612777990119442632)
XLA Ops:
  7.3 13.8 %project.1 = (bf16[512,512]{1,0:T(8,128)(2,1)S(1)}, bf16[512,256]{1,0:T(8,128)(2,1)S(1)}, bf16[128,768]{1,0:T(8,128)(2,1)S(1)}, bf16[128,768]{1,0:T(8,128)(2,1)S(1)}, bf16[128,768]{1,0:T(8,128)(2,1)S(1)}) custom-call(s32[2]{0:T(128)S(1)} %pad_add_fusion.place_ref, bf16[512,4096]{1,0:T(8,128)(2,1)} %x_ref.2, bf16[4096,512]{1,0:T(8,128)(2,1)} %refs_7_.1, ...), custom_call_target="tpu_custom_call" | custom-call | flops 3221225472 | bytes 10485760 | tf_op jit(solution)/shard_map/project/pallas_call | solution.py:93
  21.1 3.1 %collective-permute-start.3 = (bf16[128,768]{1,0:T(8,128)(2,1)S(1)}, bf16[128,768]{1,0:T(8,128)(2,1)S(1)}, u32[]{:S(2)}, u32[]{:S(2)}) collective-permute-start(bf16[128,768]{1,0:T(8,128)(2,1)S(1)} %get-tuple-element.48), channel_id=1, source_target_pairs={{0,1},{1,2},{2,3},{3,0},{4,5},{5,6},{6,7},{7,4},{8,9},{9,10},{10,1... | collective-permute-start | bytes 589832 | tf_op jit(solution)/shard_map/ppermute | solution.py:388
  24.2 1.5 collective-permute-start
  25.6 3.9 %collective-permute-start.1 = (bf16[512,256]{1,0:T(8,128)(2,1)S(1)}, bf16[512,256]{1,0:T(8,128)(2,1)S(1)}, u32[]{:S(2)}, u32[]{:S(2)}) collective-permute-start(bf16[512,256]{1,0:T(8,128)(2,1)S(1)} %get-tuple-element.52.kv0), channel_id=1, source_target_pairs={{0,8},{4,12},{8,16},{12,20},{16,24},{20,28},{1,9},{5,13},{9,17},{1... | collective-permute-start | bytes 786440 | tf_op jit(solution)/shard_map/ppermute | solution.py:379
  29.5 4.3 %collective-permute-start.2 = (bf16[512,256]{1,0:T(8,128)(2,1)S(1)}, bf16[512,256]{1,0:T(8,128)(2,1)S(1)}, u32[]{:S(2)}, u32[]{:S(2)}) collective-permute-start(bf16[512,256]{1,0:T(8,128)(2,1)S(1)} %get-tuple-element.52.kv0), channel_id=1, source_target_pairs={{0,12},{4,16},{8,20},{12,24},{16,28},{1,13},{5,17},{9,21},{13,25},... | collective-permute-start | bytes 786440 | tf_op jit(solution)/shard_map/ppermute | solution.py:379
  33.8 2.7 %collective-permute-start.4 = (bf16[128,768]{1,0:T(8,128)(2,1)S(1)}, bf16[128,768]{1,0:T(8,128)(2,1)S(1)}, u32[]{:S(2)}, u32[]{:S(2)}) collective-permute-start(bf16[128,768]{1,0:T(8,128)(2,1)S(1)} %get-tuple-element.49), channel_id=1, source_target_pairs={{0,2},{1,3},{2,0},{3,1},{4,6},{5,7},{6,4},{7,5},{8,10},{9,11},{10,... | collective-permute-start | bytes 589832 | tf_op jit(solution)/shard_map/ppermute | solution.py:388
  36.5 1.3 collective-permute-start.5
  37.8 8.4 %collective-permute-done.4 = bf16[128,768]{1,0:T(8,128)(2,1)S(1)} collective-permute-done((bf16[128,768]{1,0:T(8,128)(2,1)S(1)}, bf16[128,768]{1,0:T(8,128)(2,1)S(1)}, u32[]{:S(2)}, u32[]{:S(2)}) %collective-permute-start.4) | collective-permute-done | bytes 196640 | tf_op jit(solution)/shard_map/ppermute | solution.py:388
  46.2 0.9 pad_maximum_fusion
  47.4 0.2 select_reduce_fusion
  47.6 7.2 %attention.1 = (bf16[512,512]{1,0:T(8,128)(2,1)}, bf16[512,512]{1,0:T(8,128)(2,1)S(1)}, bf16[512,512]{1,0:T(8,128)(2,1)S(1)}, f32[512,256]{1,0:T(8,128)S(1)}, bf...) custom-call(s32[4]{0:T(128)S(1)} %broadcast_subtract_fusion.first_ref, ...), custom_call_target="tpu_custom_call" | custom-call | flops 6442450944 | bytes 6291456 | tf_op jit(solution)/shard_map/attention/pallas_call | solution.py:357
  54.7 3.6 %collective-permute-start.9 = (bf16[512,512]{1,0:T(8,128)(2,1)S(1)}, bf16[512,512]{1,0:T(8,128)(2,1)S(1)}, u32[]{:S(2)}, u32[]{:S(2)}) collective-permute-start(bf16[512,512]{1,0:T(8,128)(2,1)S(1)} %get-tuple-element.67.refs_3_), channel_id=1, source_target_pairs={{0,1},{1,2},{2,3},{3,0},{4,5},{5,6},{6,7},{7,4},{8,9},{9,10},{10,1... | collective-permute-start | bytes 1572872 | tf_op jit(solution)/shard_map/ppermute | solution.py:388
  58.4 1.3 collective-permute-start.6
  59.7 1.3 collective-permute-start.7
  61.0 1.3 collective-permute-start.8
  62.3 5.2 %collective-permute-done.6.refs_0_ = bf16[512,256]{1,0:T(8,128)(2,1)S(1)} collective-permute-done((bf16[512,256]{1,0:T(8,128)(2,1)S(1)}, bf16[512,256]{1,0:T(8,128)(2,1)S(1)}, u32[]{:S(2)}, u32[]{:S(2)}) %collective-permute-start.6) | collective-permute-done | bytes 262176 | tf_op jit(solution)/shard_map/ppermute | solution.py:379
  67.5 9.1 %collective-permute-done.7.refs_1_ = bf16[512,256]{1,0:T(8,128)(2,1)S(1)} collective-permute-done((bf16[512,256]{1,0:T(8,128)(2,1)S(1)}, bf16[512,256]{1,0:T(8,128)(2,1)S(1)}, u32[]{:S(2)}, u32[]{:S(2)}) %collective-permute-start.7) | collective-permute-done | bytes 262176 | tf_op jit(solution)/shard_map/ppermute | solution.py:379
  76.6 14.6 %collective-permute-done.8.refs_2_ = bf16[512,256]{1,0:T(8,128)(2,1)S(1)} collective-permute-done((bf16[512,256]{1,0:T(8,128)(2,1)S(1)}, bf16[512,256]{1,0:T(8,128)(2,1)S(1)}, u32[]{:S(2)}, u32[]{:S(2)}) %collective-permute-start.8) | collective-permute-done | bytes 262176 | tf_op jit(solution)/shard_map/ppermute | solution.py:379
  91.2 0.2 combine.1
  91.5 2.1 %collective-permute-start.13 = (bf16[512,768]{1,0:T(8,128)(2,1)S(1)}, bf16[512,768]{1,0:T(8,128)(2,1)S(1)}, u32[]{:S(2)}, u32[]{:S(2)}) collective-permute-start(bf16[512,768]{1,0:T(8,128)(2,1)S(1)} %get-tuple-element.73.refs_1_.refs_2_.refs_3_), channel_id=1, source_target_pairs={{0,3},{1,0},{2,1},{3,2},{4,7},{5,4},{6,5},{7,6},{8,11},{9,8},{10,9... | collective-permute-start | bytes 2359304 | tf_op jit(solution)/shard_map/ppermute | solution.py:388
  93.7 0.2 collective-permute-done.14.other_joined_ref
  93.9 2.2 %copy-done = bf16[512,4096]{1,0:T(8,128)(2,1)S(1)} copy-done((bf16[512,4096]{1,0:T(8,128)(2,1)S(1)}, bf16[512,4096]{1,0:T(8,128)(2,1)}, u32[]{:S(2)}) %copy-start) | copy-done | bytes 4194328
  96.1 6.3 %weight_terms.1 = (f32[768,512]{1,0:T(8,128)S(1)}, bf16[768,512]{1,0:T(8,128)(2,1)S(1)}, bf16[768,512]{1,0:T(8,128)(2,1)S(1)}, bf16[768,512]{1,0:T(8,128)(2,1)S(1)}) custom-call(s32[4]{0:T(128)S(1)} %multiply_add_fusion.index_ref, bf16[768,512]{1,0:T(8,128)(2,1)S(1)} %get-tuple-element.74.joined_ref, ...), custom_call_target="tpu_custom_call" | custom-call | flops 3221225472 | bytes 10485760 | tf_op jit(solution)/shard_map/weight_terms/pallas_call | solution.py:158
  102.4 11.1 %collective-permute-start.16 = (bf16[768,512]{1,0:T(8,128)(2,1)S(1)}, bf16[768,512]{1,0:T(8,128)(2,1)S(1)}, u32[]{:S(2)}, u32[]{:S(2)}) collective-permute-start(bf16[768,512]{1,0:T(8,128)(2,1)S(1)} %get-tuple-element.77), channel_id=1, source_target_pairs={{0,8},{4,12},{8,0},{12,4},{16,24},{20,28},{24,16},{28,20},{1,9},{5... | collective-permute-start | bytes 2359304 | tf_op jit(solution)/shard_map/ppermute | solution.py:383
  113.6 1.5 collective-permute-start.18
  115.2 9.7 %collective-permute-done.11.refs_5_ = bf16[512,256]{1,0:T(8,128)(2,1)S(1)} collective-permute-done((bf16[512,256]{1,0:T(8,128)(2,1)S(1)}, bf16[512,256]{1,0:T(8,128)(2,1)S(1)}, u32[]{:S(2)}, u32[]{:S(2)}) %collective-permute-start.11) | collective-permute-done | bytes 262176 | tf_op jit(solution)/shard_map/ppermute | solution.py:388
  124.9 1.0 collective-permute-start.12
  125.9 6.0 %collective-permute-done.16.refs_1_ = bf16[768,512]{1,0:T(8,128)(2,1)S(1)} collective-permute-done((bf16[768,512]{1,0:T(8,128)(2,1)S(1)}, bf16[768,512]{1,0:T(8,128)(2,1)S(1)}, u32[]{:S(2)}, u32[]{:S(2)}) %collective-permute-start.16) | collective-permute-done | bytes 786464 | tf_op jit(solution)/shard_map/ppermute | solution.py:383
  131.9 18.0 %collective-permute-done.17.refs_2_ = bf16[768,512]{1,0:T(8,128)(2,1)S(1)} collective-permute-done((bf16[768,512]{1,0:T(8,128)(2,1)S(1)}, bf16[768,512]{1,0:T(8,128)(2,1)S(1)}, u32[]{:S(2)}, u32[]{:S(2)}) %collective-permute-start.17) | collective-permute-done | bytes 786464 | tf_op jit(solution)/shard_map/ppermute | solution.py:383
  149.9 1.5 weight_rows.1
  151.4 5.3 %products_near.1.refs_5_ = f32[512,1024]{1,0:T(8,128)S(1)} custom-call(s32[1]{0:T(128)} %bitcast.2.refs_0_, bf16[512,768]{1,0:T(8,128)(2,1)S(1)} %get-tuple-element.73.refs_1_.refs_2_.refs_3_, bf16[512,768]{1,0:T(8,128)(2,1)S(1)} %get-tuple-element.73.refs_1_.refs_2_.refs_3_, bf16[512,768]{1,0:T(8,128)(2,1)S(1)} %get-tuple-element.73.refs_1_.refs_2_.refs_3_, ...), custom_call_target="tpu_custom_call" | custom-call | flops 2415919104 | bytes 8388608 | tf_op jit(solution)/shard_map/products_near/pallas_call | solution.py:245
  156.8 4.2 %products_far.1 = bf16[512,1024]{1,0:T(8,128)(2,1)} custom-call(s32[1]{0:T(128)} %bitcast.2.refs_0_, bf16[512,512]{1,0:T(8,128)(2,1)S(1)} %collective-permute-done.10.refs_1_, bf16[512,256]{1,0:T(8,128)(2,1)S(1)} %collective-permute-done.12.refs_2_, bf16[8,3,128,768]{3,2,1,0:T(8,128)(2,1)} %bitcast.8, bf16[8,3,128,768]{3,2,1,0:T(8,128)(2,1)} %bitcast.9, ...), custom_call_target="tpu_custom_call" | custom-call | flops 805306368 | bytes 8388608 | tf_op jit(solution)/shard_map/products_far/pallas_call | solution.py:245
  (29 shorter events, 0.6 us)
Async XLA Ops:
  7.2 144.3 %all-gather.2.cloned.1.call-start = ((), (), s32[]{:S(2)}) async-start(), calls=%async_computation | async-start | bytes 5308416 | tf_op jit(solution)/shard_map/all_gather | solution.py:410
  21.1 26.1 %copy-start.2 = (s32[8]{0:T(128)S(1)}, s32[8]{0:T(128)}, u32[]{:S(2)}) copy-start(s32[8]{0:T(128)} %param.11) | copy-start | bytes 100
  21.1 26.5 %copy-start.1 = (bf16[512,512]{1,0:T(8,128)(2,1)S(1)}, bf16[512,512]{1,0:T(8,128)(2,1)}, u32[]{:S(2)}) copy-start(bf16[512,512]{1,0:T(8,128)(2,1)} %grad_ref.1) | copy-start | bytes 1572868
  21.1 15.4 %collective-permute-start.3 = (bf16[128,768]{1,0:T(8,128)(2,1)S(1)}, bf16[128,768]{1,0:T(8,128)(2,1)S(1)}, u32[]{:S(2)}, u32[]{:S(2)}) collective-permute-start(bf16[128,768]{1,0:T(8,128)(2,1)S(1)} %get-tuple-element.48), channel_id=1, source_target_pairs={{0,1},{1,2},{2,3},{3,0},{4,5},{5,6},{6,7},{7,4},{8,9},{9,10},{10,1... | collective-permute-start | bytes 589832 | tf_op jit(solution)/shard_map/ppermute | solution.py:388
  24.2 22.1 %collective-permute-start = (bf16[512,256]{1,0:T(8,128)(2,1)S(1)}, bf16[512,256]{1,0:T(8,128)(2,1)S(1)}, u32[]{:S(2)}, u32[]{:S(2)}) collective-permute-start(bf16[512,256]{1,0:T(8,128)(2,1)S(1)} %get-tuple-element.52.kv0), channel_id=1, source_target_pairs={{0,4},{4,8},{8,12},{12,16},{16,20},{20,24},{24,28},{1,5},{5,9},{9,... | collective-permute-start | bytes 786440 | tf_op jit(solution)/shard_map/ppermute | solution.py:379
  25.6 20.6 %collective-permute-start.1 = (bf16[512,256]{1,0:T(8,128)(2,1)S(1)}, bf16[512,256]{1,0:T(8,128)(2,1)S(1)}, u32[]{:S(2)}, u32[]{:S(2)}) collective-permute-start(bf16[512,256]{1,0:T(8,128)(2,1)S(1)} %get-tuple-element.52.kv0), channel_id=1, source_target_pairs={{0,8},{4,12},{8,16},{12,20},{16,24},{20,28},{1,9},{5,13},{9,17},{1... | collective-permute-start | bytes 786440 | tf_op jit(solution)/shard_map/ppermute | solution.py:379
  29.5 16.7 %collective-permute-start.2 = (bf16[512,256]{1,0:T(8,128)(2,1)S(1)}, bf16[512,256]{1,0:T(8,128)(2,1)S(1)}, u32[]{:S(2)}, u32[]{:S(2)}) collective-permute-start(bf16[512,256]{1,0:T(8,128)(2,1)S(1)} %get-tuple-element.52.kv0), channel_id=1, source_target_pairs={{0,12},{4,16},{8,20},{12,24},{16,28},{1,13},{5,17},{9,21},{13,25},... | collective-permute-start | bytes 786440 | tf_op jit(solution)/shard_map/ppermute | solution.py:379
  33.8 12.4 %collective-permute-start.4 = (bf16[128,768]{1,0:T(8,128)(2,1)S(1)}, bf16[128,768]{1,0:T(8,128)(2,1)S(1)}, u32[]{:S(2)}, u32[]{:S(2)}) collective-permute-start(bf16[128,768]{1,0:T(8,128)(2,1)S(1)} %get-tuple-element.49), channel_id=1, source_target_pairs={{0,2},{1,3},{2,0},{3,1},{4,6},{5,7},{6,4},{7,5},{8,10},{9,11},{10,... | collective-permute-start | bytes 589832 | tf_op jit(solution)/shard_map/ppermute | solution.py:388
  36.5 9.7 %collective-permute-start.5 = (bf16[128,768]{1,0:T(8,128)(2,1)S(1)}, bf16[128,768]{1,0:T(8,128)(2,1)S(1)}, u32[]{:S(2)}, u32[]{:S(2)}) collective-permute-start(bf16[128,768]{1,0:T(8,128)(2,1)S(1)} %get-tuple-element.50), channel_id=1, source_target_pairs={{0,3},{1,0},{2,1},{3,2},{4,7},{5,4},{6,5},{7,6},{8,11},{9,8},{10,9... | collective-permute-start | bytes 589832 | tf_op jit(solution)/shard_map/ppermute | solution.py:388
  47.1 46.8 %collective-permute-start.15 = (bf16[512,4096]{1,0:T(8,128)(2,1)}, bf16[512,4096]{1,0:T(8,128)(2,1)}, u32[]{:S(2)}, u32[]{:S(2)}) collective-permute-start(bf16[512,4096]{1,0:T(8,128)(2,1)} %x_ref.2), channel_id=1, source_target_pairs={{0,4},{4,0},{8,12},{12,8},{16,20},{20,16},{24,28},{28,24},{1,5},{5... | collective-permute-start | bytes 12582920 | tf_op jit(solution)/shard_map/ppermute | solution.py:383
  54.7 36.5 %collective-permute-start.9 = (bf16[512,512]{1,0:T(8,128)(2,1)S(1)}, bf16[512,512]{1,0:T(8,128)(2,1)S(1)}, u32[]{:S(2)}, u32[]{:S(2)}) collective-permute-start(bf16[512,512]{1,0:T(8,128)(2,1)S(1)} %get-tuple-element.67.refs_3_), channel_id=1, source_target_pairs={{0,1},{1,2},{2,3},{3,0},{4,5},{5,6},{6,7},{7,4},{8,9},{9,10},{10,1... | collective-permute-start | bytes 1572872 | tf_op jit(solution)/shard_map/ppermute | solution.py:388
  58.4 9.1 %collective-permute-start.6 = (bf16[512,256]{1,0:T(8,128)(2,1)S(1)}, bf16[512,256]{1,0:T(8,128)(2,1)S(1)}, u32[]{:S(2)}, u32[]{:S(2)}) collective-permute-start(bf16[512,256]{1,0:T(8,128)(2,1)S(1)} %get-tuple-element.57), channel_id=1, source_target_pairs={{4,0},{8,4},{12,8},{16,12},{20,16},{24,20},{28,24},{5,1},{9,5},{13... | collective-permute-start | bytes 786440 | tf_op jit(solution)/shard_map/ppermute | solution.py:379
  59.7 16.9 %collective-permute-start.7 = (bf16[512,256]{1,0:T(8,128)(2,1)S(1)}, bf16[512,256]{1,0:T(8,128)(2,1)S(1)}, u32[]{:S(2)}, u32[]{:S(2)}) collective-permute-start(bf16[512,256]{1,0:T(8,128)(2,1)S(1)} %get-tuple-element.58), channel_id=1, source_target_pairs={{8,0},{12,4},{16,8},{20,12},{24,16},{28,20},{9,1},{13,5},{17,9},{2... | collective-permute-start | bytes 786440 | tf_op jit(solution)/shard_map/ppermute | solution.py:379
  61.0 30.2 %collective-permute-start.8 = (bf16[512,256]{1,0:T(8,128)(2,1)S(1)}, bf16[512,256]{1,0:T(8,128)(2,1)S(1)}, u32[]{:S(2)}, u32[]{:S(2)}) collective-permute-start(bf16[512,256]{1,0:T(8,128)(2,1)S(1)} %get-tuple-element.59), channel_id=1, source_target_pairs={{12,0},{16,4},{20,8},{24,12},{28,16},{13,1},{17,5},{21,9},{25,13},... | collective-permute-start | bytes 786440 | tf_op jit(solution)/shard_map/ppermute | solution.py:379
  91.4 2.5 %collective-permute-start.14 = (bf16[768,512]{1,0:T(8,128)(2,1)S(1)}, bf16[768,512]{1,0:T(8,128)(2,1)}, u32[]{:S(2)}, u32[]{:S(2)}) collective-permute-start(bf16[768,512]{1,0:T(8,128)(2,1)S(1)} %get-tuple-element.74.joined_ref), channel_id=1, source_target_pairs={{0,4},{4,0},{8,12},{12,8},{16,20},{20,16},{24,28},{28,24},{1,5},{5... | collective-permute-start | bytes 2359304 | tf_op jit(solution)/shard_map/ppermute | solution.py:383
  91.5 33.4 %collective-permute-start.13 = (bf16[512,768]{1,0:T(8,128)(2,1)S(1)}, bf16[512,768]{1,0:T(8,128)(2,1)S(1)}, u32[]{:S(2)}, u32[]{:S(2)}) collective-permute-start(bf16[512,768]{1,0:T(8,128)(2,1)S(1)} %get-tuple-element.73.refs_1_.refs_2_.refs_3_), channel_id=1, source_target_pairs={{0,3},{1,0},{2,1},{3,2},{4,7},{5,4},{6,5},{7,6},{8,11},{9,8},{10,9... | collective-permute-start | bytes 2359304 | tf_op jit(solution)/shard_map/ppermute | solution.py:388
  93.9 2.2 %copy-start = (bf16[512,4096]{1,0:T(8,128)(2,1)S(1)}, bf16[512,4096]{1,0:T(8,128)(2,1)}, u32[]{:S(2)}) copy-start(bf16[512,4096]{1,0:T(8,128)(2,1)} %x_ref.2) | copy-start | bytes 12582916
  102.4 29.5 %collective-permute-start.16 = (bf16[768,512]{1,0:T(8,128)(2,1)S(1)}, bf16[768,512]{1,0:T(8,128)(2,1)S(1)}, u32[]{:S(2)}, u32[]{:S(2)}) collective-permute-start(bf16[768,512]{1,0:T(8,128)(2,1)S(1)} %get-tuple-element.77), channel_id=1, source_target_pairs={{0,8},{4,12},{8,0},{12,4},{16,24},{20,28},{24,16},{28,20},{1,9},{5... | collective-permute-start | bytes 2359304 | tf_op jit(solution)/shard_map/ppermute | solution.py:383
  113.6 36.4 %collective-permute-start.17 = (bf16[768,512]{1,0:T(8,128)(2,1)S(1)}, bf16[768,512]{1,0:T(8,128)(2,1)S(1)}, u32[]{:S(2)}, u32[]{:S(2)}) collective-permute-start(bf16[768,512]{1,0:T(8,128)(2,1)S(1)} %get-tuple-element.78), channel_id=1, source_target_pairs={{0,16},{4,20},{8,24},{12,28},{16,0},{20,4},{24,8},{28,12},{1,17},{... | collective-permute-start | bytes 2359304 | tf_op jit(solution)/shard_map/ppermute | solution.py:383
  113.6 36.4 %collective-permute-start.18 = (bf16[768,512]{1,0:T(8,128)(2,1)S(1)}, bf16[768,512]{1,0:T(8,128)(2,1)S(1)}, u32[]{:S(2)}, u32[]{:S(2)}) collective-permute-start(bf16[768,512]{1,0:T(8,128)(2,1)S(1)} %get-tuple-element.79), channel_id=1, source_target_pairs={{0,24},{4,28},{8,16},{12,20},{16,8},{20,12},{24,0},{28,4},{1,25},{... | collective-permute-start | bytes 2359304 | tf_op jit(solution)/shard_map/ppermute | solution.py:383
  115.1 9.8 %collective-permute-start.11 = (bf16[512,256]{1,0:T(8,128)(2,1)S(1)}, bf16[512,256]{1,0:T(8,128)(2,1)S(1)}, u32[]{:S(2)}, u32[]{:S(2)}) collective-permute-start(bf16[512,256]{1,0:T(8,128)(2,1)S(1)} %get-tuple-element.69), channel_id=1, source_target_pairs={{0,1},{1,2},{2,3},{3,0},{4,5},{5,6},{6,7},{7,4},{8,9},{9,10},{10,1... | collective-permute-start | bytes 786440 | tf_op jit(solution)/shard_map/ppermute | solution.py:388
  124.9 31.9 %collective-permute-start.10 = (bf16[512,512]{1,0:T(8,128)(2,1)S(1)}, bf16[512,512]{1,0:T(8,128)(2,1)S(1)}, u32[]{:S(2)}, u32[]{:S(2)}) collective-permute-start(bf16[512,512]{1,0:T(8,128)(2,1)S(1)} %collective-permute-done.9.refs_4_), channel_id=1, source_target_pairs={{0,1},{1,2},{2,3},{3,0},{4,5},{5,6},{6,7},{7,4},{8,9},{9,10},{10,1... | collective-permute-start | bytes 1572872 | tf_op jit(solution)/shard_map/ppermute | solution.py:388
  124.9 31.8 %collective-permute-start.12 = (bf16[512,256]{1,0:T(8,128)(2,1)S(1)}, bf16[512,256]{1,0:T(8,128)(2,1)S(1)}, u32[]{:S(2)}, u32[]{:S(2)}) collective-permute-start(bf16[512,256]{1,0:T(8,128)(2,1)S(1)} %collective-permute-done.11.refs_5_), channel_id=1, source_target_pairs={{0,1},{1,2},{2,3},{3,0},{4,5},{5,6},{6,7},{7,4},{8,9},{9,10},{10,1... | collective-permute-start | bytes 786440 | tf_op jit(solution)/shard_map/ppermute | solution.py:388
Sparse Core Ops, SparseCore 0:
  47.2 47.8 all-gather.1
